TPU v7x, 32 devices: a whole 2x2x4 slice. The times are simulated.
32 devices in a mesh: blk: 8 (over z, x), wn: 4 (over y, core).
Axes of the slice: x: 2, y: 2, z: 4, core: 2. Of those that a mesh axis runs over, the one named last changes fastest.
Arguments:
- species_molar_share: float32 [11, 64, 2, 1024], P(None, 'wn', None, 'blk'), may hold values from 0.01 to 1
- flow_speed_vector: float32 [2, 64, 2, 1024], P(None, 'wn', None, 'blk'), may hold values from -6 to 6
- thermal_level: float32 [64, 2, 1024], P('wn', None, 'blk'), may hold values from 0.5 to 2
- shear_collision_terms: float32 [11, 11], replicated, may hold values from 1 to 2
- thermal_collision_terms: float32 [11, 11], replicated, may hold values from 1 to 2
Outputs:
- final_state: float32 [14, 64, 2, 1024], P(None, 'wn', None, 'blk')
- last_residual: float32 [14, 64, 2, 1024], P(None, 'wn', None, 'blk')
All inputs are finite; a program needn't handle non-finite values.
Results may differ from a plain program's by a relative error of at most 0.00005.
Values sent between devices are 32-bit elements; how exact they have to be, the bound alone decides.
A program may use at most 64 MiB of HBM per device.

v0:
```python
import jax
import jax.numpy as jnp
import numpy as np
from jax import lax
from jax.sharding import PartitionSpec as P

MASSES = np.array([28.0, 32.0, 30.0, 14.0, 16.0, 28.0, 32.0, 30.0, 14.0, 16.0, 0.00055]) / 28.0


def extended(block, sides, width):
    for axis, dim in sides:
        count = lax.axis_size(axis)
        forward = [(i, i + 1) for i in range(count - 1)]
        backward = [(target, source) for source, target in forward]
        low = lax.ppermute(
            lax.slice_in_dim(block, block.shape[dim] - width, None, axis=dim), axis, forward
        )
        high = lax.ppermute(lax.slice_in_dim(block, 0, width, axis=dim), axis, backward)
        block = jnp.concatenate([low, block, high], axis=dim)
    return block


def properties(padded, shear_collision_terms, thermal_collision_terms):
    fractions = padded[:11]
    heat = padded[13]
    denom_visc = jnp.einsum(
        "sr,rjki->sjki", shear_collision_terms, fractions, precision=lax.Precision.HIGHEST
    )
    denom_cond = jnp.einsum(
        "sr,rjki->sjki", thermal_collision_terms, fractions, precision=lax.Precision.HIGHEST
    )
    mixture_viscosity = heat**0.7 * jnp.sum(
        fractions * MASSES[:, None, None, None] / denom_visc, axis=0
    )
    conduct = heat**0.5 * jnp.sum(fractions / denom_cond, axis=0)
    return (mixture_viscosity, conduct)


def shifted(field, down, across):
    rows = field.shape[-3]
    cols = field.shape[-1]
    return field[..., 1 + down : rows - 1 + down, :, 1 + across : cols - 1 + across]


def diffuse(padded, coeff):
    center_c = shifted(coeff, 0, 0)
    center_face = shifted(padded, 0, 0)
    total = jnp.zeros_like(center_face)
    for down, across in ((1, 0), (-1, 0), (0, 1), (0, -1)):
        total = total + 0.5 * (center_c + shifted(coeff, down, across)) * (
            shifted(padded, down, across) - center_face
        )
    return total


def residual_of(padded, mixture_viscosity, conduct):
    return jnp.concatenate(
        [
            diffuse(padded[:11], conduct),
            diffuse(padded[11:13], mixture_viscosity),
            diffuse(padded[13:], conduct),
        ],
        axis=0,
    )


def assemble(payload, row_ext, col_ext):
    wn_here = lax.axis_index("wn")
    wn_count = lax.axis_size("wn")
    blk_here = lax.axis_index("blk")
    blk_count = lax.axis_size("blk")
    bottom = jnp.where(wn_here == 0, payload[:, 1:2, ::-1, :], row_ext[:, :1])
    top = jnp.where(wn_here == wn_count - 1, payload[:, -1:], row_ext[:, -1:])
    left = jnp.where(blk_here == 0, payload[..., :1], col_ext[..., :1])
    right = jnp.where(blk_here == blk_count - 1, payload[:, :, ::-1, -1:], col_ext[..., -1:])
    middle = jnp.concatenate([left, payload, right], axis=3)
    edge_pad = ((0, 0), (0, 0), (0, 0), (1, 1))
    return jnp.concatenate([jnp.pad(bottom, edge_pad), middle, jnp.pad(top, edge_pad)], axis=1)


def evaluate(state, shear_collision_terms, thermal_collision_terms):
    mixture_viscosity, conduct = properties(state, shear_collision_terms, thermal_collision_terms)
    payload = jnp.concatenate([state, mixture_viscosity[None], conduct[None]], axis=0)
    row_ext = extended(payload, (("wn", 1),), 1)
    col_ext = extended(payload, (("blk", 3),), 1)
    padded = assemble(payload, row_ext, col_ext)
    return residual_of(padded[:14], padded[14], padded[15])


def local(
    species_molar_share,
    flow_speed_vector,
    thermal_level,
    shear_collision_terms,
    thermal_collision_terms,
):
    step = 0.16
    first_position = jnp.concatenate(
        [species_molar_share, flow_speed_vector, thermal_level[None]], axis=0
    )
    first = first_position + step * evaluate(
        first_position, shear_collision_terms, thermal_collision_terms
    )
    second = 0.75 * first_position + 0.25 * (
        first + step * evaluate(first, shear_collision_terms, thermal_collision_terms)
    )
    last_residual = evaluate(second, shear_collision_terms, thermal_collision_terms)
    final_state = first_position / 3.0 + 2.0 / 3.0 * (second + step * last_residual)
    return (final_state, last_residual)


def solution(mesh):
    return jax.shard_map(
        local,
        mesh=mesh,
        in_specs=(
            P(None, "wn", None, "blk"),
            P(None, "wn", None, "blk"),
            P("wn", None, "blk"),
            P(),
            P(),
        ),
        out_specs=(P(None, "wn", None, "blk"), P(None, "wn", None, "blk")),
        check_vma=False,
    )
```

profile of v0, /device:TPU:14, one launch (start us, length us, event | category | flops | bytes accessed | tf_op | source)
XLA Modules:
  0.0 77.5 jit_solution(7860356899075355458)
XLA Ops:
  0.6 0.0 copy-start
  0.7 1.5 %fusion = f32[16,2,128]{2,1,0:T(2,128)S(1)} fusion(f32[11,16,2,128]{3,2,1,0:T(2,128)} %param.8, f32[11,11]{1,0:T(8,128)} %param.12), kind=kOutput, calls=%fused_computation.1 | convolution fusion | flops 6033408 | bytes 197092 | tf_op jit(solution)/shard_map/sr,rjki->sjki/dot_general | solution.py:29
  2.2 0.4 fusion.10
  2.6 0.2 copy-done.5
  2.8 0.1 fusion.146
  3.0 0.6 copy-done.3
  3.6 0.7 copy-done.2
  4.4 0.1 slice.550
  4.5 3.5 %collective-permute-start.1 = (f32[16,16,2,1]{3,1,2,0:T(8,128)S(1)}, f32[16,16,2,1]{3,1,2,0:T(8,128)S(1)}, u32[]{:S(2)}, u32[]{:S(2)}) collective-permute-start(f32[16,16,2,1]{3,1,2,0:T(8,128)S(1)} %slice.550), channel_id=1, source_target_pairs={{0,4},{4,8},{8,12},{12,16},{16,20},{20,24},{24,28},{1,5},{5,9},{9,... | collective-permute-start | bytes 6152 | tf_op jit(solution)/shard_map/ppermute | solution.py:15
  8.0 1.9 %collective-permute-start.3 = (f32[16,1,2,128]{3,1,2,0:T(1,128)S(1)}, f32[16,1,2,128]{3,1,2,0:T(1,128)S(1)}, u32[]{:S(2)}, u32[]{:S(2)}) collective-permute-start(f32[16,1,2,128]{3,1,2,0:T(1,128)S(1)} %slice.551), channel_id=1, source_target_pairs={{1,0},{2,1},{3,2},{5,4},{6,5},{7,6},{9,8},{10,9},{11,10},{13,12},{... | collective-permute-start | bytes 49160 | tf_op jit(solution)/shard_map/ppermute | solution.py:18
  9.9 4.5 %collective-permute-done.1 = f32[16,16,2,1]{3,1,2,0:T(8,128)S(1)} collective-permute-done((f32[16,16,2,1]{3,1,2,0:T(8,128)S(1)}, f32[16,16,2,1]{3,1,2,0:T(8,128)S(1)}, u32[]{:S(2)}, u32[]{:S(2)}) %collective-permute-start.1) | collective-permute-done | bytes 2080 | tf_op jit(solution)/shard_map/ppermute | solution.py:15
  14.5 3.3 %collective-permute-start.2 = (f32[16,16,2,1]{3,1,2,0:T(8,128)S(1)}, f32[16,16,2,1]{3,1,2,0:T(8,128)S(1)}, u32[]{:S(2)}, u32[]{:S(2)}) collective-permute-start(f32[16,16,2,1]{3,1,2,0:T(8,128)S(1)} %get-tuple-element.52), channel_id=1, source_target_pairs={{4,0},{8,4},{12,8},{16,12},{20,16},{24,20},{28,24},{5,1},{9,5},{13... | collective-permute-start | bytes 6152 | tf_op jit(solution)/shard_map/ppermute | solution.py:18
  17.9 1.9 %collective-permute-start = (f32[16,1,2,128]{3,1,2,0:T(1,128)S(1)}, f32[16,1,2,128]{3,1,2,0:T(1,128)S(1)}, u32[]{:S(2)}, u32[]{:S(2)}) collective-permute-start(f32[16,1,2,128]{3,1,2,0:T(1,128)S(1)} %get-tuple-element.50), channel_id=1, source_target_pairs={{0,1},{1,2},{2,3},{4,5},{5,6},{6,7},{8,9},{9,10},{10,11},{12,13},{... | collective-permute-start | bytes 49160 | tf_op jit(solution)/shard_map/ppermute | solution.py:15
  19.8 4.6 %collective-permute-done.2 = f32[16,16,2,1]{3,1,2,0:T(8,128)S(1)} collective-permute-done((f32[16,16,2,1]{3,1,2,0:T(8,128)S(1)}, f32[16,16,2,1]{3,1,2,0:T(8,128)S(1)}, u32[]{:S(2)}, u32[]{:S(2)}) %collective-permute-start.2) | collective-permute-done | bytes 2080 | tf_op jit(solution)/shard_map/ppermute | solution.py:18
  24.5 0.1 pad.20
  24.6 0.1 pad.19
  24.8 0.1 fusion.48
  24.9 0.1 fusion.120
  25.0 0.1 fusion.108
  25.1 0.1 fusion.70
  25.2 0.4 fusion.19
  25.7 0.5 fusion.7
  26.2 0.2 copy-done.4
  26.4 0.5 fusion.5
  26.9 0.2 fusion.44
  27.2 0.1 slice.573
  27.3 3.5 %collective-permute-start.5 = (f32[16,16,2,1]{3,1,2,0:T(8,128)S(1)}, f32[16,16,2,1]{3,1,2,0:T(8,128)S(1)}, u32[]{:S(2)}, u32[]{:S(2)}) collective-permute-start(f32[16,16,2,1]{3,1,2,0:T(8,128)S(1)} %slice.573), channel_id=1, source_target_pairs={{0,4},{4,8},{8,12},{12,16},{16,20},{20,24},{24,28},{1,5},{5,9},{9,... | collective-permute-start | bytes 6152 | tf_op jit(solution)/shard_map/ppermute | solution.py:15
  30.8 4.8 %collective-permute-done.5 = f32[16,16,2,1]{3,1,2,0:T(8,128)S(1)} collective-permute-done((f32[16,16,2,1]{3,1,2,0:T(8,128)S(1)}, f32[16,16,2,1]{3,1,2,0:T(8,128)S(1)}, u32[]{:S(2)}, u32[]{:S(2)}) %collective-permute-start.5) | collective-permute-done | bytes 2080 | tf_op jit(solution)/shard_map/ppermute | solution.py:15
  35.6 3.3 %collective-permute-start.6 = (f32[16,16,2,1]{3,1,2,0:T(8,128)S(1)}, f32[16,16,2,1]{3,1,2,0:T(8,128)S(1)}, u32[]{:S(2)}, u32[]{:S(2)}) collective-permute-start(f32[16,16,2,1]{3,1,2,0:T(8,128)S(1)} %get-tuple-element.47), channel_id=1, source_target_pairs={{4,0},{8,4},{12,8},{16,12},{20,16},{24,20},{28,24},{5,1},{9,5},{13... | collective-permute-start | bytes 6152 | tf_op jit(solution)/shard_map/ppermute | solution.py:18
  39.0 1.9 %collective-permute-start.7 = (f32[16,1,2,128]{3,1,2,0:T(1,128)S(1)}, f32[16,1,2,128]{3,1,2,0:T(1,128)S(1)}, u32[]{:S(2)}, u32[]{:S(2)}) collective-permute-start(f32[16,1,2,128]{3,1,2,0:T(1,128)S(1)} %get-tuple-element.46), channel_id=1, source_target_pairs={{1,0},{2,1},{3,2},{5,4},{6,5},{7,6},{9,8},{10,9},{11,10},{13,12},{... | collective-permute-start | bytes 49160 | tf_op jit(solution)/shard_map/ppermute | solution.py:18
  40.9 3.9 %collective-permute-done.6 = f32[16,16,2,1]{3,1,2,0:T(8,128)S(1)} collective-permute-done((f32[16,16,2,1]{3,1,2,0:T(8,128)S(1)}, f32[16,16,2,1]{3,1,2,0:T(8,128)S(1)}, u32[]{:S(2)}, u32[]{:S(2)}) %collective-permute-start.6) | collective-permute-done | bytes 2080 | tf_op jit(solution)/shard_map/ppermute | solution.py:18
  44.9 1.9 %collective-permute-start.4 = (f32[16,1,2,128]{3,1,2,0:T(1,128)S(1)}, f32[16,1,2,128]{3,1,2,0:T(1,128)S(1)}, u32[]{:S(2)}, u32[]{:S(2)}) collective-permute-start(f32[16,1,2,128]{3,1,2,0:T(1,128)S(1)} %get-tuple-element.25), channel_id=1, source_target_pairs={{0,1},{1,2},{2,3},{4,5},{5,6},{6,7},{8,9},{9,10},{10,11},{12,13},{... | collective-permute-start | bytes 49160 | tf_op jit(solution)/shard_map/ppermute | solution.py:15
  46.8 0.2 pad_maximum_fusion
  47.0 0.1 pad.22
  47.1 2.8 %collective-permute-done.4 = f32[16,1,2,128]{3,1,2,0:T(1,128)S(1)} collective-permute-done((f32[16,1,2,128]{3,1,2,0:T(1,128)S(1)}, f32[16,1,2,128]{3,1,2,0:T(1,128)S(1)}, u32[]{:S(2)}, u32[]{:S(2)}) %collective-permute-start.4) | collective-permute-done | bytes 16416 | tf_op jit(solution)/shard_map/ppermute | solution.py:15
  49.9 0.1 pad.21
  50.1 0.1 fusion.47
  50.2 0.1 fusion.101
  50.3 0.1 fusion.90
  50.4 0.1 fusion.61
  50.5 0.3 fusion.32
  50.8 0.1 fusion.15
  50.9 0.5 fusion.3
  51.4 0.5 fusion.1
  51.9 0.2 fusion.45
  52.2 0.1 slice.590
  52.3 3.4 %collective-permute-start.9 = (f32[16,16,2,1]{3,1,2,0:T(8,128)S(1)}, f32[16,16,2,1]{3,1,2,0:T(8,128)S(1)}, u32[]{:S(2)}, u32[]{:S(2)}) collective-permute-start(f32[16,16,2,1]{3,1,2,0:T(8,128)S(1)} %slice.590), channel_id=1, source_target_pairs={{0,4},{4,8},{8,12},{12,16},{16,20},{20,24},{24,28},{1,5},{5,9},{9,... | collective-permute-start | bytes 6152 | tf_op jit(solution)/shard_map/ppermute | solution.py:15
  55.8 4.8 %collective-permute-done.9 = f32[16,16,2,1]{3,1,2,0:T(8,128)S(1)} collective-permute-done((f32[16,16,2,1]{3,1,2,0:T(8,128)S(1)}, f32[16,16,2,1]{3,1,2,0:T(8,128)S(1)}, u32[]{:S(2)}, u32[]{:S(2)}) %collective-permute-start.9) | collective-permute-done | bytes 2080 | tf_op jit(solution)/shard_map/ppermute | solution.py:15
  60.6 3.3 %collective-permute-start.10 = (f32[16,16,2,1]{3,1,2,0:T(8,128)S(1)}, f32[16,16,2,1]{3,1,2,0:T(8,128)S(1)}, u32[]{:S(2)}, u32[]{:S(2)}) collective-permute-start(f32[16,16,2,1]{3,1,2,0:T(8,128)S(1)} %get-tuple-element.41), channel_id=1, source_target_pairs={{4,0},{8,4},{12,8},{16,12},{20,16},{24,20},{28,24},{5,1},{9,5},{13... | collective-permute-start | bytes 6152 | tf_op jit(solution)/shard_map/ppermute | solution.py:18
  64.0 1.9 %collective-permute-start.11 = (f32[16,1,2,128]{3,1,2,0:T(1,128)S(1)}, f32[16,1,2,128]{3,1,2,0:T(1,128)S(1)}, u32[]{:S(2)}, u32[]{:S(2)}) collective-permute-start(f32[16,1,2,128]{3,1,2,0:T(1,128)S(1)} %get-tuple-element.40), channel_id=1, source_target_pairs={{1,0},{2,1},{3,2},{5,4},{6,5},{7,6},{9,8},{10,9},{11,10},{13,12},{... | collective-permute-start | bytes 49160 | tf_op jit(solution)/shard_map/ppermute | solution.py:18
  65.9 3.9 %collective-permute-done.10 = f32[16,16,2,1]{3,1,2,0:T(8,128)S(1)} collective-permute-done((f32[16,16,2,1]{3,1,2,0:T(8,128)S(1)}, f32[16,16,2,1]{3,1,2,0:T(8,128)S(1)}, u32[]{:S(2)}, u32[]{:S(2)}) %collective-permute-start.10) | collective-permute-done | bytes 2080 | tf_op jit(solution)/shard_map/ppermute | solution.py:18
  69.9 1.9 %collective-permute-start.8 = (f32[16,1,2,128]{3,1,2,0:T(1,128)S(1)}, f32[16,1,2,128]{3,1,2,0:T(1,128)S(1)}, u32[]{:S(2)}, u32[]{:S(2)}) collective-permute-start(f32[16,1,2,128]{3,1,2,0:T(1,128)S(1)} %get-tuple-element.18), channel_id=1, source_target_pairs={{0,1},{1,2},{2,3},{4,5},{5,6},{6,7},{8,9},{9,10},{10,11},{12,13},{... | collective-permute-start | bytes 49160 | tf_op jit(solution)/shard_map/ppermute | solution.py:15
  71.8 0.2 pad_maximum_fusion.1
  72.0 0.1 pad.24
  72.2 2.8 %collective-permute-done.8 = f32[16,1,2,128]{3,1,2,0:T(1,128)S(1)} collective-permute-done((f32[16,1,2,128]{3,1,2,0:T(1,128)S(1)}, f32[16,1,2,128]{3,1,2,0:T(1,128)S(1)}, u32[]{:S(2)}, u32[]{:S(2)}) %collective-permute-start.8) | collective-permute-done | bytes 16416 | tf_op jit(solution)/shard_map/ppermute | solution.py:15
  75.0 0.1 pad.23
  75.1 0.1 fusion.46
  75.2 0.1 fusion.84
  75.3 0.1 fusion.73
  75.4 0.1 fusion.54
  75.6 0.3 fusion.25
  75.8 0.1 pad_maximum_fusion.5
  75.9 0.8 %copy.111 = f32[14,16,2,128]{3,2,1,0:T(2,128)} copy(f32[14,16,2,128]{3,1,2,0:T(8,128)S(1)} %get-tuple-element.54) | data formatting | bytes 458752
  76.7 0.8 %copy.110 = f32[14,16,2,128]{3,2,1,0:T(2,128)} copy(f32[14,16,2,128]{3,1,2,0:T(8,128)S(1)} %get-tuple-element.55) | data formatting | bytes 458752
  (38 shorter events, 0.7 us)
Async XLA Ops:
  0.6 1.5 %copy-start = (f32[11,11]{1,0:T(8,128)S(1)}, f32[11,11]{1,0:T(8,128)}, u32[]{:S(2)}) copy-start(f32[11,11]{1,0:T(8,128)} %param.11) | copy-start | bytes 1456
  0.6 1.5 %copy-start.1 = (f32[11,16,2,128]{3,2,1,0:T(2,128)S(1)}, f32[11,16,2,128]{3,2,1,0:T(2,128)}, u32[]{:S(2)}) copy-start(f32[11,16,2,128]{3,2,1,0:T(2,128)} %param.8) | copy-start | bytes 540676
  2.2 0.7 copy-start.5
  2.8 0.8 copy-start.3
  3.6 0.7 copy-start.2
  4.5 9.9 %collective-permute-start.1 = (f32[16,16,2,1]{3,1,2,0:T(8,128)S(1)}, f32[16,16,2,1]{3,1,2,0:T(8,128)S(1)}, u32[]{:S(2)}, u32[]{:S(2)}) collective-permute-start(f32[16,16,2,1]{3,1,2,0:T(8,128)S(1)} %slice.550), channel_id=1, source_target_pairs={{0,4},{4,8},{8,12},{12,16},{16,20},{20,24},{24,28},{1,5},{5,9},{9,... | collective-permute-start | bytes 6152 | tf_op jit(solution)/shard_map/ppermute | solution.py:15
  8.0 9.9 %collective-permute-start.3 = (f32[16,1,2,128]{3,1,2,0:T(1,128)S(1)}, f32[16,1,2,128]{3,1,2,0:T(1,128)S(1)}, u32[]{:S(2)}, u32[]{:S(2)}) collective-permute-start(f32[16,1,2,128]{3,1,2,0:T(1,128)S(1)} %slice.551), channel_id=1, source_target_pairs={{1,0},{2,1},{3,2},{5,4},{6,5},{7,6},{9,8},{10,9},{11,10},{13,12},{... | collective-permute-start | bytes 49160 | tf_op jit(solution)/shard_map/ppermute | solution.py:18
  14.5 10.0 %collective-permute-start.2 = (f32[16,16,2,1]{3,1,2,0:T(8,128)S(1)}, f32[16,16,2,1]{3,1,2,0:T(8,128)S(1)}, u32[]{:S(2)}, u32[]{:S(2)}) collective-permute-start(f32[16,16,2,1]{3,1,2,0:T(8,128)S(1)} %get-tuple-element.52), channel_id=1, source_target_pairs={{4,0},{8,4},{12,8},{16,12},{20,16},{24,20},{28,24},{5,1},{9,5},{13... | collective-permute-start | bytes 6152 | tf_op jit(solution)/shard_map/ppermute | solution.py:18
  17.9 6.7 %collective-permute-start = (f32[16,1,2,128]{3,1,2,0:T(1,128)S(1)}, f32[16,1,2,128]{3,1,2,0:T(1,128)S(1)}, u32[]{:S(2)}, u32[]{:S(2)}) collective-permute-start(f32[16,1,2,128]{3,1,2,0:T(1,128)S(1)} %get-tuple-element.50), channel_id=1, source_target_pairs={{0,1},{1,2},{2,3},{4,5},{5,6},{6,7},{8,9},{9,10},{10,11},{12,13},{... | collective-permute-start | bytes 49160 | tf_op jit(solution)/shard_map/ppermute | solution.py:15
  25.7 0.7 copy-start.4
  27.3 8.3 %collective-permute-start.5 = (f32[16,16,2,1]{3,1,2,0:T(8,128)S(1)}, f32[16,16,2,1]{3,1,2,0:T(8,128)S(1)}, u32[]{:S(2)}, u32[]{:S(2)}) collective-permute-start(f32[16,16,2,1]{3,1,2,0:T(8,128)S(1)} %slice.573), channel_id=1, source_target_pairs={{0,4},{4,8},{8,12},{12,16},{16,20},{20,24},{24,28},{1,5},{5,9},{9,... | collective-permute-start | bytes 6152 | tf_op jit(solution)/shard_map/ppermute | solution.py:15
  35.6 9.2 %collective-permute-start.6 = (f32[16,16,2,1]{3,1,2,0:T(8,128)S(1)}, f32[16,16,2,1]{3,1,2,0:T(8,128)S(1)}, u32[]{:S(2)}, u32[]{:S(2)}) collective-permute-start(f32[16,16,2,1]{3,1,2,0:T(8,128)S(1)} %get-tuple-element.47), channel_id=1, source_target_pairs={{4,0},{8,4},{12,8},{16,12},{20,16},{24,20},{28,24},{5,1},{9,5},{13... | collective-permute-start | bytes 6152 | tf_op jit(solution)/shard_map/ppermute | solution.py:18
  39.0 5.8 %collective-permute-start.7 = (f32[16,1,2,128]{3,1,2,0:T(1,128)S(1)}, f32[16,1,2,128]{3,1,2,0:T(1,128)S(1)}, u32[]{:S(2)}, u32[]{:S(2)}) collective-permute-start(f32[16,1,2,128]{3,1,2,0:T(1,128)S(1)} %get-tuple-element.46), channel_id=1, source_target_pairs={{1,0},{2,1},{3,2},{5,4},{6,5},{7,6},{9,8},{10,9},{11,10},{13,12},{... | collective-permute-start | bytes 49160 | tf_op jit(solution)/shard_map/ppermute | solution.py:18
  44.9 5.1 %collective-permute-start.4 = (f32[16,1,2,128]{3,1,2,0:T(1,128)S(1)}, f32[16,1,2,128]{3,1,2,0:T(1,128)S(1)}, u32[]{:S(2)}, u32[]{:S(2)}) collective-permute-start(f32[16,1,2,128]{3,1,2,0:T(1,128)S(1)} %get-tuple-element.25), channel_id=1, source_target_pairs={{0,1},{1,2},{2,3},{4,5},{5,6},{6,7},{8,9},{9,10},{10,11},{12,13},{... | collective-permute-start | bytes 49160 | tf_op jit(solution)/shard_map/ppermute | solution.py:15
  52.3 8.3 %collective-permute-start.9 = (f32[16,16,2,1]{3,1,2,0:T(8,128)S(1)}, f32[16,16,2,1]{3,1,2,0:T(8,128)S(1)}, u32[]{:S(2)}, u32[]{:S(2)}) collective-permute-start(f32[16,16,2,1]{3,1,2,0:T(8,128)S(1)} %slice.590), channel_id=1, source_target_pairs={{0,4},{4,8},{8,12},{12,16},{16,20},{20,24},{24,28},{1,5},{5,9},{9,... | collective-permute-start | bytes 6152 | tf_op jit(solution)/shard_map/ppermute | solution.py:15
  60.6 9.2 %collective-permute-start.10 = (f32[16,16,2,1]{3,1,2,0:T(8,128)S(1)}, f32[16,16,2,1]{3,1,2,0:T(8,128)S(1)}, u32[]{:S(2)}, u32[]{:S(2)}) collective-permute-start(f32[16,16,2,1]{3,1,2,0:T(8,128)S(1)} %get-tuple-element.41), channel_id=1, source_target_pairs={{4,0},{8,4},{12,8},{16,12},{20,16},{24,20},{28,24},{5,1},{9,5},{13... | collective-permute-start | bytes 6152 | tf_op jit(solution)/shard_map/ppermute | solution.py:18
  64.0 5.8 %collective-permute-start.11 = (f32[16,1,2,128]{3,1,2,0:T(1,128)S(1)}, f32[16,1,2,128]{3,1,2,0:T(1,128)S(1)}, u32[]{:S(2)}, u32[]{:S(2)}) collective-permute-start(f32[16,1,2,128]{3,1,2,0:T(1,128)S(1)} %get-tuple-element.40), channel_id=1, source_target_pairs={{1,0},{2,1},{3,2},{5,4},{6,5},{7,6},{9,8},{10,9},{11,10},{13,12},{... | collective-permute-start | bytes 49160 | tf_op jit(solution)/shard_map/ppermute | solution.py:18
  69.9 5.1 %collective-permute-start.8 = (f32[16,1,2,128]{3,1,2,0:T(1,128)S(1)}, f32[16,1,2,128]{3,1,2,0:T(1,128)S(1)}, u32[]{:S(2)}, u32[]{:S(2)}) collective-permute-start(f32[16,1,2,128]{3,1,2,0:T(1,128)S(1)} %get-tuple-element.18), channel_id=1, source_target_pairs={{0,1},{1,2},{2,3},{4,5},{5,6},{6,7},{8,9},{9,10},{10,11},{12,13},{... | collective-permute-start | bytes 49160 | tf_op jit(solution)/shard_map/ppermute | solution.py:15
where the time goes:
time: 78.1 us; the launch traced here: 77.5 us
  waiting for transfers between devices  32 us (41%)
  starting transfers between devices  31.9 us (41%)
  local copies, waits for them, and re-layouts  4.52 us (6%)
  matrix products  3.94 us (5%)
  other arithmetic  3.93 us (5%)
  between operations  1.22 us (2%)
    ppermute x6, waiting for transfers between devices, extended(): lax.ppermute(lax.slice_in_dim(block, block.shape[dim] - width, None, axis...  19.7 us
    ppermute x6, starting transfers between devices, extended(): lax.ppermute(lax.slice_in_dim(block, block.shape[dim] - width, None, axis...  16.1 us
    ppermute x6, starting transfers between devices, extended(): lax.ppermute(lax.slice_in_dim(block, 0, width, axis=dim), axis, backward)  15.8 us
    ppermute x6, waiting for transfers between devices, extended(): lax.ppermute(lax.slice_in_dim(block, 0, width, axis=dim), axis, backward)  12.4 us
    unnamed x17, local copies, waits for them, and re-layouts  3.36 us
    dot_general x3, matrix products, properties(): jnp.einsum('sr,rjki->sjki', thermal_collision_terms, fractions, precision...  2.49 us
    add x9, other arithmetic, diffuse(): total + 0.5 * (center_c + shifted(coeff, down, across)) * (shifted(padded...  1.62 us
  transfers between devices with their start and end apart: 12, of which 8 were waited for; matrix products, arithmetic and copies ran while one was open for 1% of the time, Pallas kernels for 0%

commit v1 on v0

v1 whole, which is shorter than its diff:
```python
import jax
import jax.numpy as jnp
import numpy as np
from jax import lax
from jax.experimental import pallas as pl
from jax.experimental.pallas import tpu as pltpu
from jax.sharding import PartitionSpec as P

MASSES = np.array([28.0, 32.0, 30.0, 14.0, 16.0, 28.0, 32.0, 30.0, 14.0, 16.0, 0.00055]) / 28.0
NS = 11
NV = 14
STEP = 0.16
VERTICAL = ((1, 0), (-1, 0))
SIDEWAYS = ((0, 1), (0, -1), (1, 1), (1, -1), (-1, 1), (-1, -1))
EDGE_TILES = 4


def roll(x, shift, axis):
    size = x.shape[axis]
    shift = shift % size
    return x if shift == 0 else pltpu.roll(x, shift, axis)


def lanes_of(shape):
    return lax.broadcasted_iota(jnp.int32, shape, len(shape) - 1)


def rows_of(shape):
    return lax.broadcasted_iota(jnp.int32, shape, len(shape) - 2)


def exchange_kernel(
    species, velocity, heat, vert, side, own, out_v, send_v, recv_v, send_s, recv_s
):
    wn = lax.axis_index("wn")
    blk = lax.axis_index("blk")
    wn_count = lax.axis_size("wn")
    blk_count = lax.axis_size("blk")

    def exists(dw, db):
        checks = []
        if dw:
            checks.append(wn < wn_count - 1 if dw > 0 else wn > 0)
        if db:
            checks.append(blk < blk_count - 1 if db > 0 else blk > 0)
        return checks[0] if len(checks) == 1 else jnp.logical_and(*checks)

    def device(dw, db):
        return {"wn": wn + dw, "blk": blk + db}

    barrier = pltpu.get_barrier_semaphore()
    for dw, db in VERTICAL + SIDEWAYS:

        @pl.when(exists(dw, db))
        def _(dw=dw, db=db):
            pl.semaphore_signal(
                barrier, inc=1, device_id=device(dw, db), device_id_type=pl.DeviceIdType.MESH
            )

    def tile(v, g):
        rows = pl.ds(8 * g, 8)
        if v < NS:
            return species[v, rows]
        if v < NS + 2:
            return velocity[v - NS, rows]
        return heat[rows]

    slot = lanes_of((8, 128)) // 8
    for t in range(EDGE_TILES):
        packed = jnp.zeros((8, 128), jnp.float32)
        for v in range(4 * t, min(4 * t + 4, NV)):
            for g in range(4):
                at = 4 * (v % 4) + g
                packed = jnp.where(slot == at, roll(tile(v, g), 8 * at + 3, 1), packed)
        own[t] = packed
        out_v[0, NV + t] = packed
        out_v[1, NV + t] = packed
    for v in range(NV):
        out_v[0, v] = tile(v, 3)
        out_v[1, v] = tile(v, 0)

    along_wn = 1 + (wn > 0).astype(jnp.int32) + (wn < wn_count - 1).astype(jnp.int32)
    along_blk = 1 + (blk > 0).astype(jnp.int32) + (blk < blk_count - 1).astype(jnp.int32)
    pl.semaphore_wait(barrier, along_wn * along_blk - 1)

    copies = []
    for n, (dw, db) in enumerate(VERTICAL):
        copies.append((dw, db, pltpu.make_async_remote_copy(
            src_ref=out_v.at[n], dst_ref=vert.at[n], send_sem=send_v.at[n], recv_sem=recv_v.at[n],
            device_id=device(dw, db), device_id_type=pl.DeviceIdType.MESH)))
    for n, (dw, db) in enumerate(SIDEWAYS):
        copies.append((dw, db, pltpu.make_async_remote_copy(
            src_ref=own, dst_ref=side.at[n], send_sem=send_s.at[n], recv_sem=recv_s.at[n],
            device_id=device(dw, db), device_id_type=pl.DeviceIdType.MESH)))
    for dw, db, copy in copies:
        pl.when(exists(dw, db))(copy.start)
    for dw, db, copy in copies:
        pl.when(exists(-dw, -db))(copy.wait_recv)
    for dw, db, copy in copies:
        pl.when(exists(dw, db))(copy.wait_send)


def sections_kernel(
    shear, thermal, species, velocity, heat, vert, side, own, final, residual, now, first, kept
):
    wn = lax.axis_index("wn")
    blk = lax.axis_index("blk")
    at_bottom = wn == 0
    at_top = wn == lax.axis_size("wn") - 1
    at_wake = blk == 0
    at_nose = blk == lax.axis_size("blk") - 1
    lane = lanes_of((8, 128))
    sub = rows_of((8, 128))
    c = lane % 8
    is_left = lane < 64
    group = (lane % 64) // 8

    for v in range(NV):
        now[v, 0:8] = vert[0, v]
        now[v, 40:48] = vert[1, v]
    now[0:NS, 8:40] = species[...]
    now[NS:NS + 2, 8:40] = velocity[...]
    now[NV - 1, 8:40] = heat[...]
    for t in range(EDGE_TILES):
        from_left, from_right = c < 3, c >= 3
        mid, low, high = own[t], vert[0, NV + t], vert[1, NV + t]
        left_mid = jnp.where(from_left, side[0, t], mid)
        left_low = jnp.where(from_left, side[2, t], low)
        left_high = jnp.where(from_left, side[4, t], high)
        right_mid = jnp.where(from_right, side[1, t], mid)
        right_low = jnp.where(from_right, side[3, t], low)
        right_high = jnp.where(from_right, side[5, t], high)
        for v in range(4 * t, min(4 * t + 4, NV)):
            base = 32 * (v % 4)
            left = roll(left_mid, 8 - base, 1)
            left = jnp.where(group == 0, roll(left_low, -24 - base, 1), left)
            left = jnp.where(group == 5, roll(left_high, 40 - base, 1), left)
            right = roll(right_mid, 72 - base, 1)
            right = jnp.where(group == 0, roll(right_low, 40 - base, 1), right)
            right = jnp.where(group == 5, roll(right_high, 104 - base, 1), right)
            now[v, 48:56] = jnp.where(is_left, left, right)
    first[...] = now[...]

    bottom_6 = (sub == 6) & at_bottom
    bottom_7 = (sub == 7) & at_bottom
    top_01 = (sub < 2) & at_top
    patch_bottom_6 = bottom_6 & (group == 0)
    patch_bottom_7 = bottom_7 & (group == 0)
    patch_top = top_01 & (group == 5)
    patch_wake = is_left & (c == 2) & at_wake
    patch_nose = (~is_left) & (c == 3) & at_nose
    even = sub % 2 == 0

    def ghost(v):
        inner = now[v, 8:16]
        below = now[v, 0:8]
        below = jnp.where(bottom_6, roll(inner, 3, 0), below)
        now[v, 0:8] = jnp.where(bottom_7, roll(inner, 5, 0), below)
        now[v, 40:48] = jnp.where(top_01, roll(now[v, 32:40], 2, 0), now[v, 40:48])
        patch = now[v, 48:56]
        inner = roll(patch, -8, 1)
        patch = jnp.where(patch_bottom_6, roll(inner, 3, 0), patch)
        patch = jnp.where(patch_bottom_7, roll(inner, 5, 0), patch)
        patch = jnp.where(patch_top, roll(roll(patch, 8, 1), 2, 0), patch)
        patch = jnp.where(patch_wake, roll(patch, -1, 1), patch)
        inner = roll(patch, 1, 1)
        patch = jnp.where(
            patch_nose, jnp.where(even, roll(inner, -1, 0), roll(inner, 1, 0)), patch
        )
        now[v, 48:56] = patch

    def patch_up(x):
        y = roll(x, -2, 0)
        return jnp.where(sub < 6, y, roll(y, -8, 1))

    def patch_down(x):
        y = roll(x, 2, 0)
        return jnp.where(sub >= 2, y, roll(y, 8, 1))

    main_lane = lanes_of((48, 128))
    last_lane = main_lane == 127
    zero_lane = main_lane == 0

    def section(number, old_share, new_share):
        for v in range(NV):
            ghost(v)
        visc = jnp.zeros((56, 128), jnp.float32)
        cond = jnp.zeros((56, 128), jnp.float32)
        for s in range(NS):
            den_visc = shear[s, 0] * now[0]
            den_cond = thermal[s, 0] * now[0]
            for r in range(1, NS):
                den_visc = den_visc + shear[s, r] * now[r]
                den_cond = den_cond + thermal[s, r] * now[r]
            visc = visc + (float(MASSES[s]) * now[s]) / den_visc
            cond = cond + now[s] / den_cond
        temperature = now[NV - 1]
        kept[0] = jnp.exp(0.7 * jnp.log(temperature)) * visc
        kept[1] = jnp.sqrt(temperature) * cond
        for n in range(2):
            main, patch = kept[n, 0:48], kept[n, 48:56]
            kept[2 + n, 0:48] = 0.5 * (main + roll(main, -2, 0))
            kept[2 + n, 48:56] = 0.5 * (patch + patch_up(patch))
            kept[4 + n, 0:48] = 0.5 * (main + roll(main, -1, 1))
            kept[4 + n, 48:56] = 0.5 * (patch + roll(patch, -1, 1))
        for v in range(NV):
            n = 0 if NS <= v < NS + 2 else 1
            main, patch = now[v, 0:48], now[v, 48:56]
            across_patch = kept[4 + n, 48:56] * (roll(patch, -1, 1) - patch)
            seam = jnp.where(c == 1, roll(across_patch, 63, 1), across_patch)
            closing = jnp.concatenate([roll(seam, -8 * g - 2, 1) for g in range(6)], axis=0)
            across = kept[4 + n, 0:48] * (roll(main, -1, 1) - main)
            before = jnp.where(zero_lane, closing, roll(across, 1, 1))
            across = jnp.where(last_lane, closing, across)
            down = kept[2 + n, 0:48] * (roll(main, -2, 0) - main)
            change = (across - before) + (down - roll(down, 2, 0))
            if number < 2:
                down_patch = kept[2 + n, 48:56] * (patch_up(patch) - patch)
                change_patch = (across_patch - roll(across_patch, 1, 1)) + (
                    down_patch - patch_down(down_patch)
                )
                new_main = main + STEP * change
                new_patch = patch + STEP * change_patch
                if old_share:
                    new_main = old_share * first[v, 0:48] + new_share * new_main
                    new_patch = old_share * first[v, 48:56] + new_share * new_patch
                now[v, 0:48] = new_main
                now[v, 48:56] = new_patch
            else:
                inner = change[8:40]
                residual[v] = inner
                final[v] = old_share * first[v, 8:40] + new_share * (main[8:40] + STEP * inner)

    section(0, 0.0, 1.0)
    section(1, 0.75, 0.25)
    section(2, 1.0 / 3.0, 2.0 / 3.0)


def local(species, velocity, heat, shear, thermal):
    layers = species.shape[1]
    columns = species.shape[3]
    assert (layers, columns) == (16, 128)
    rows = 2 * layers
    species = species.reshape(NS, rows, columns)
    velocity = velocity.reshape(2, rows, columns)
    heat = heat.reshape(rows, columns)
    f32 = jnp.float32
    vmem = pl.BlockSpec(memory_space=pltpu.VMEM)
    smem = pl.BlockSpec(memory_space=pltpu.SMEM)
    tiles = NV + EDGE_TILES
    vert, side, own = pl.pallas_call(
        exchange_kernel,
        out_shape=(
            jax.ShapeDtypeStruct((2, tiles, 8, columns), f32),
            jax.ShapeDtypeStruct((6, EDGE_TILES, 8, columns), f32),
            jax.ShapeDtypeStruct((EDGE_TILES, 8, columns), f32),
        ),
        in_specs=[vmem] * 3,
        out_specs=(vmem,) * 3,
        scratch_shapes=[
            pltpu.VMEM((2, tiles, 8, columns), f32),
            pltpu.SemaphoreType.DMA((2,)),
            pltpu.SemaphoreType.DMA((2,)),
            pltpu.SemaphoreType.DMA((6,)),
            pltpu.SemaphoreType.DMA((6,)),
        ],
        compiler_params=pltpu.CompilerParams(collective_id=0, has_side_effects=True),
        name="exchange",
    )(species, velocity, heat)
    shape = jax.ShapeDtypeStruct((NV, rows, columns), f32)
    final, residual = pl.pallas_call(
        sections_kernel,
        out_shape=(shape, shape),
        in_specs=[smem] * 2 + [vmem] * 6,
        out_specs=(vmem,) * 2,
        scratch_shapes=[
            pltpu.VMEM((NV, rows + 24, columns), f32),
            pltpu.VMEM((NV, rows + 24, columns), f32),
            pltpu.VMEM((6, rows + 24, columns), f32),
        ],
        name="sections",
    )(shear, thermal, species, velocity, heat, vert, side, own)
    whole = (NV, layers, 2, columns)
    return final.reshape(whole), residual.reshape(whole)


def solution(mesh):
    return jax.shard_map(
        local,
        mesh=mesh,
        in_specs=(
            P(None, "wn", None, "blk"),
            P(None, "wn", None, "blk"),
            P("wn", None, "blk"),
            P(),
            P(),
        ),
        out_specs=(P(None, "wn", None, "blk"), P(None, "wn", None, "blk")),
        check_vma=False,
    )
```

time: 78.1 us -> 15.7 us (0.20)
  the two profiles are of different devices: /device:TPU:14 before, /device:TPU:0 now
where the time goes in v1:
time: 15.7 us; the launch traced here: 15.5 us
  Pallas kernels  14.9 us (95%)
  between operations  0.64 us (4%)
    pallas_call x1, Pallas kernels, local(): pl.pallas_call(exchange_kernel, out_shape=(jax.ShapeDtypeStruct((2, tiles...  8.74 us
    pallas_call x1, Pallas kernels, local(): pl.pallas_call(sections_kernel, out_shape=(shape, shape), in_specs=[smem]...  6.13 us

profile of v1, /device:TPU:0, one launch (start us, length us, event | category | flops | bytes accessed | tf_op | source)
XLA Modules:
  0.0 15.5 jit_solution(14966098855815805535)
XLA Ops:
  0.6 8.7 %exchange.1 = (f32[2,18,8,128]{3,2,1,0:T(8,128)}, f32[6,4,8,128]{3,2,1,0:T(8,128)}, f32[4,8,128]{2,1,0:T(8,128)}) custom-call(f32[11,32,128]{2,1,0:T(8,128)} %bitcast.5, f32[2,32,128]{2,1,0:T(8,128)} %bitcast.7, f32[32,128]{1,0:T(8,128)} %bitcast.9), custom_call_target="tpu_custom_call" | custom-call | tf_op jit(solution)/shard_map/exchange/pallas_call | solution.py:251
  9.4 6.1 %sections.1 = (f32[14,32,128]{2,1,0:T(8,128)}, f32[14,32,128]{2,1,0:T(8,128)}) custom-call(f32[11,11]{1,0:T(8,128)} %shear.1, f32[11,11]{1,0:T(8,128)} %thermal.1, f32[11,32,128]{2,1,0:T(8,128)} %bitcast.6, f32[2,32,128]{2,1,0:T(8,128)} %bitcast.8, f32[32,128]{1,0:T(8,128)} %bitcast.10, f32[2,18,8,128]{3,2,1,0:T(8,128)} %get-tuple-element.7.vert, ...), custom_call_target="tpu_custom_call" | custom-call | tf_op jit(solution)/shard_map/sections/pallas_call | solution.py:271

commit v2 on v1

--- a/solution.py
+++ b/solution.py
@@ -19,6 +19,11 @@
     size = x.shape[axis]
     shift = shift % size
     return x if shift == 0 else pltpu.roll(x, shift, axis)
+
+
+def inverse(x):
+    guess = pl.reciprocal(x, approx=True)
+    return guess * (2.0 - x * guess)
 
 
 def lanes_of(shape):
@@ -184,19 +189,38 @@
     def section(number, old_share, new_share):
         for v in range(NV):
             ghost(v)
-        visc = jnp.zeros((56, 128), jnp.float32)
-        cond = jnp.zeros((56, 128), jnp.float32)
+        if number == 0:
+            cells = [now[r] for r in range(NV)]
+        else:
+            cells = [
+                jnp.concatenate(
+                    [now[r, 8:40], now[r, 48:56], jnp.where(sub >= 4, now[r, 0:8], now[r, 40:48])],
+                    axis=0,
+                )
+                for r in range(NV)
+            ]
+        visc = cond = None
         for s in range(NS):
-            den_visc = shear[s, 0] * now[0]
-            den_cond = thermal[s, 0] * now[0]
+            den_visc = shear[s, 0] * cells[0]
+            den_cond = thermal[s, 0] * cells[0]
             for r in range(1, NS):
-                den_visc = den_visc + shear[s, r] * now[r]
-                den_cond = den_cond + thermal[s, r] * now[r]
-            visc = visc + (float(MASSES[s]) * now[s]) / den_visc
-            cond = cond + now[s] / den_cond
-        temperature = now[NV - 1]
-        kept[0] = jnp.exp(0.7 * jnp.log(temperature)) * visc
-        kept[1] = jnp.sqrt(temperature) * cond
+                den_visc = den_visc + shear[s, r] * cells[r]
+                den_cond = den_cond + thermal[s, r] * cells[r]
+            visc_s = (float(MASSES[s]) * cells[s]) * inverse(den_visc)
+            cond_s = cells[s] * inverse(den_cond)
+            visc = visc_s if s == 0 else visc + visc_s
+            cond = cond_s if s == 0 else cond + cond_s
+        temperature = cells[NV - 1]
+        visc = jnp.exp(0.7 * jnp.log(temperature)) * visc
+        cond = jnp.sqrt(temperature) * cond
+        for n, k in enumerate((visc, cond)):
+            if number == 0:
+                kept[n] = k
+            else:
+                kept[n, 8:40] = k[0:32]
+                kept[n, 48:56] = k[32:40]
+                kept[n, 0:8] = k[40:48]
+                kept[n, 40:48] = k[40:48]
         for n in range(2):
             main, patch = kept[n, 0:48], kept[n, 48:56]
             kept[2 + n, 0:48] = 0.5 * (main + roll(main, -2, 0))

time: 15.7 us -> 15.7 us (level)
  no operation moved by 1% of the time
where the time goes in v2:
time: 15.7 us; the launch traced here: 15.5 us
  Pallas kernels  14.9 us (95%)
  between operations  0.64 us (4%)
    pallas_call x1, Pallas kernels, local(): pl.pallas_call(exchange_kernel, out_shape=(jax.ShapeDtypeStruct((2, tiles...  8.74 us
    pallas_call x1, Pallas kernels, local(): pl.pallas_call(sections_kernel, out_shape=(shape, shape), in_specs=[smem]...  6.17 us

profile of v2, /device:TPU:0, one launch (start us, length us, event | category | flops | bytes accessed | tf_op | source)
XLA Modules:
  0.0 15.5 jit_solution(6234722836110081004)
XLA Ops:
  0.6 8.7 %exchange.1 = (f32[2,18,8,128]{3,2,1,0:T(8,128)}, f32[6,4,8,128]{3,2,1,0:T(8,128)}, f32[4,8,128]{2,1,0:T(8,128)}) custom-call(f32[11,32,128]{2,1,0:T(8,128)} %bitcast.5, f32[2,32,128]{2,1,0:T(8,128)} %bitcast.7, f32[32,128]{1,0:T(8,128)} %bitcast.9), custom_call_target="tpu_custom_call" | custom-call | tf_op jit(solution)/shard_map/exchange/pallas_call | solution.py:275
  9.4 6.2 %sections.1 = (f32[14,32,128]{2,1,0:T(8,128)}, f32[14,32,128]{2,1,0:T(8,128)}) custom-call(f32[11,11]{1,0:T(8,128)} %shear.1, f32[11,11]{1,0:T(8,128)} %thermal.1, f32[11,32,128]{2,1,0:T(8,128)} %bitcast.6, f32[2,32,128]{2,1,0:T(8,128)} %bitcast.8, f32[32,128]{1,0:T(8,128)} %bitcast.10, f32[2,18,8,128]{3,2,1,0:T(8,128)} %get-tuple-element.7.vert, ...), custom_call_target="tpu_custom_call" | custom-call | tf_op jit(solution)/shard_map/sections/pallas_call | solution.py:295

commit v3 on v2

v3 whole, which is shorter than its diff:
```python
import jax
import jax.numpy as jnp
import numpy as np
from jax import lax
from jax.experimental import pallas as pl
from jax.experimental.pallas import tpu as pltpu
from jax.sharding import PartitionSpec as P

MASSES = np.array([28.0, 32.0, 30.0, 14.0, 16.0, 28.0, 32.0, 30.0, 14.0, 16.0, 0.00055]) / 28.0
NS = 11
NV = 14
STEP = 0.16
VERTICAL = ((1, 0), (-1, 0))
SIDEWAYS = ((0, 1), (0, -1), (1, 1), (1, -1), (-1, 1), (-1, -1))
EDGE_TILES = 4


def roll(x, shift, axis):
    size = x.shape[axis]
    shift = shift % size
    return x if shift == 0 else pltpu.roll(x, shift, axis)


def inverse(x):
    guess = pl.reciprocal(x, approx=True)
    return guess * (2.0 - x * guess)


def lanes_of(shape):
    return lax.broadcasted_iota(jnp.int32, shape, len(shape) - 1)


def rows_of(shape):
    return lax.broadcasted_iota(jnp.int32, shape, len(shape) - 2)


def exchange_kernel(
    species, velocity, heat, vert, side, own, cells, own_v, out_v, load, send_v, recv_v, send_s, recv_s
):
    wn = lax.axis_index("wn")
    blk = lax.axis_index("blk")
    wn_count = lax.axis_size("wn")
    blk_count = lax.axis_size("blk")

    def exists(dw, db):
        checks = []
        if dw:
            checks.append(wn < wn_count - 1 if dw > 0 else wn > 0)
        if db:
            checks.append(blk < blk_count - 1 if db > 0 else blk > 0)
        return checks[0] if len(checks) == 1 else jnp.logical_and(*checks)

    def device(dw, db):
        return {"wn": wn + dw, "blk": blk + db}

    barrier = pltpu.get_barrier_semaphore()
    for dw, db in VERTICAL + SIDEWAYS:

        @pl.when(exists(dw, db))
        def _(dw=dw, db=db):
            pl.semaphore_signal(
                barrier, inc=1, device_id=device(dw, db), device_id_type=pl.DeviceIdType.MESH
            )

    loads = [
        pltpu.make_async_copy(species, cells.at[0:NS], load.at[0]),
        pltpu.make_async_copy(velocity, cells.at[NS:NS + 2], load.at[1]),
        pltpu.make_async_copy(heat, cells.at[NV - 1], load.at[2]),
    ]
    for copy in loads:
        copy.start()
    for copy in loads:
        copy.wait()

    def tile(v, g):
        return cells[v, pl.ds(8 * g, 8)]

    slot = lanes_of((8, 128)) // 8
    for t in range(EDGE_TILES):
        packed = jnp.zeros((8, 128), jnp.float32)
        for v in range(4 * t, min(4 * t + 4, NV)):
            for g in range(4):
                at = 4 * (v % 4) + g
                packed = jnp.where(slot == at, roll(tile(v, g), 8 * at + 3, 1), packed)
        own_v[t] = packed
        out_v[0, NV + t] = packed
        out_v[1, NV + t] = packed
    for v in range(NV):
        out_v[0, v] = tile(v, 3)
        out_v[1, v] = tile(v, 0)

    along_wn = 1 + (wn > 0).astype(jnp.int32) + (wn < wn_count - 1).astype(jnp.int32)
    along_blk = 1 + (blk > 0).astype(jnp.int32) + (blk < blk_count - 1).astype(jnp.int32)
    pl.semaphore_wait(barrier, along_wn * along_blk - 1)

    copies = []
    for n, (dw, db) in enumerate(VERTICAL):
        copies.append((dw, db, pltpu.make_async_remote_copy(
            src_ref=out_v.at[n], dst_ref=vert.at[n], send_sem=send_v.at[n], recv_sem=recv_v.at[n],
            device_id=device(dw, db), device_id_type=pl.DeviceIdType.MESH)))
    for n, (dw, db) in enumerate(SIDEWAYS):
        copies.append((dw, db, pltpu.make_async_remote_copy(
            src_ref=own_v, dst_ref=side.at[n], send_sem=send_s.at[n], recv_sem=recv_s.at[n],
            device_id=device(dw, db), device_id_type=pl.DeviceIdType.MESH)))
    for dw, db, copy in copies:
        pl.when(exists(dw, db))(copy.start)
    keep = pltpu.make_async_copy(own_v, own, load.at[3])
    keep.start()
    for dw, db, copy in copies:
        pl.when(exists(-dw, -db))(copy.wait_recv)
    for dw, db, copy in copies:
        pl.when(exists(dw, db))(copy.wait_send)
    keep.wait()


def sections_kernel(
    shear, thermal, species, velocity, heat, vert, side, own, final, residual, now, first, kept,
    edges, load
):
    moves = (
        (vert.at[0, NV:], edges.at[7]),
        (vert.at[1, NV:], edges.at[8]),
        (side, edges.at[0:6]),
        (own, edges.at[6]),
        (vert.at[0, 0:NV], now.at[:, 8:16]),
        (vert.at[1, 0:NV], now.at[:, 48:56]),
        (species, now.at[0:NS, 16:48]),
        (velocity, now.at[NS:NS + 2, 16:48]),
        (heat, now.at[NV - 1, 16:48]),
    )
    copies = [pltpu.make_async_copy(a, b, load.at[n]) for n, (a, b) in enumerate(moves)]
    for copy in copies:
        copy.start()
    wn = lax.axis_index("wn")
    blk = lax.axis_index("blk")
    at_bottom = wn == 0
    at_top = wn == lax.axis_size("wn") - 1
    at_wake = blk == 0
    at_nose = blk == lax.axis_size("blk") - 1
    lane = lanes_of((8, 128))
    sub = rows_of((8, 128))
    c = lane % 8
    is_left = lane < 64
    group = (lane % 64) // 8
    for copy in copies:
        copy.wait()

    for t in range(EDGE_TILES):
        from_left, from_right = c < 3, c >= 3
        mid, low, high = edges[6, t], edges[7, t], edges[8, t]
        left_mid = jnp.where(from_left, edges[0, t], mid)
        left_low = jnp.where(from_left, edges[2, t], low)
        left_high = jnp.where(from_left, edges[4, t], high)
        right_mid = jnp.where(from_right, edges[1, t], mid)
        right_low = jnp.where(from_right, edges[3, t], low)
        right_high = jnp.where(from_right, edges[5, t], high)
        for v in range(4 * t, min(4 * t + 4, NV)):
            base = 32 * (v % 4)
            left = roll(left_mid, 8 - base, 1)
            left = jnp.where(group == 0, roll(left_low, -24 - base, 1), left)
            left = jnp.where(group == 5, roll(left_high, 40 - base, 1), left)
            right = roll(right_mid, 72 - base, 1)
            right = jnp.where(group == 0, roll(right_low, 40 - base, 1), right)
            right = jnp.where(group == 5, roll(right_high, 104 - base, 1), right)
            now[v, 0:8] = jnp.where(is_left, left, right)
    first[...] = now[...]

    patch_bottom_6 = (sub == 6) & (group == 0)
    patch_bottom_7 = (sub == 7) & (group == 0)
    patch_top = (sub < 2) & (group == 5)
    patch_wake = is_left & (c == 2)
    patch_nose = (~is_left) & (c == 3)
    even = sub % 2 == 0

    def ghosts():
        @pl.when(at_bottom)
        def _():
            for v in range(NV):
                now[v, 14:15] = now[v, 19:20]
                now[v, 15:16] = now[v, 18:19]
                patch = now[v, 0:8]
                inner = roll(patch, -8, 1)
                patch = jnp.where(patch_bottom_6, roll(inner, 3, 0), patch)
                now[v, 0:8] = jnp.where(patch_bottom_7, roll(inner, 5, 0), patch)

        @pl.when(at_top)
        def _():
            for v in range(NV):
                now[v, 48:50] = now[v, 46:48]
                patch = now[v, 0:8]
                now[v, 0:8] = jnp.where(patch_top, roll(roll(patch, 8, 1), 2, 0), patch)

        @pl.when(at_wake)
        def _():
            for v in range(NV):
                patch = now[v, 0:8]
                now[v, 0:8] = jnp.where(patch_wake, roll(patch, -1, 1), patch)

        @pl.when(at_nose)
        def _():
            for v in range(NV):
                patch = now[v, 0:8]
                inner = roll(patch, 1, 1)
                inner = jnp.where(even, roll(inner, -1, 0), roll(inner, 1, 0))
                now[v, 0:8] = jnp.where(patch_nose, inner, patch)

    def patch_up(x):
        y = roll(x, -2, 0)
        return jnp.where(sub < 6, y, roll(y, -8, 1))

    def patch_down(x):
        y = roll(x, 2, 0)
        return jnp.where(sub >= 2, y, roll(y, 8, 1))

    def section(number, old_share, new_share):
        ghosts()
        if number == 0:
            cells = [now[r, 0:56] for r in range(NV)]
        else:
            cells = [
                jnp.concatenate(
                    [now[r, 0:8], now[r, 16:48], jnp.where(sub >= 4, now[r, 8:16], now[r, 48:56])],
                    axis=0,
                )
                for r in range(NV)
            ]
        visc = cond = None
        for s in range(NS):
            den_visc = shear[s, 0] * cells[0]
            den_cond = thermal[s, 0] * cells[0]
            for r in range(1, NS):
                den_visc = den_visc + shear[s, r] * cells[r]
                den_cond = den_cond + thermal[s, r] * cells[r]
            visc_s = (float(MASSES[s]) * cells[s]) * inverse(den_visc)
            cond_s = cells[s] * inverse(den_cond)
            visc = visc_s if s == 0 else visc + visc_s
            cond = cond_s if s == 0 else cond + cond_s
        temperature = cells[NV - 1]
        visc = jnp.exp(0.7 * jnp.log(temperature)) * visc
        cond = jnp.sqrt(temperature) * cond
        for n, k in enumerate((visc, cond)):
            if number == 0:
                kept[n, 0:56] = k
            else:
                kept[n, 0:8] = k[0:8]
                kept[n, 16:48] = k[8:40]
                kept[n, 8:16] = k[40:48]
                kept[n, 48:56] = k[40:48]
        for n in range(2):
            main, patch = kept[n, 8:56], kept[n, 0:8]
            kept[2 + n, 8:56] = 0.5 * (main + kept[n, 10:58])
            kept[2 + n, 0:8] = 0.5 * (patch + patch_up(patch))
            kept[4 + n, 8:56] = 0.5 * (main + roll(main, -1, 1))
            kept[4 + n, 0:8] = 0.5 * (patch + roll(patch, -1, 1))
        low, count = (8, 48) if number < 2 else (16, 32)
        here, after, ahead = pl.ds(low, count), pl.ds(low + 2, count), pl.ds(low - 2, count)
        last_lane = lanes_of((count, 128)) == 127
        zero_lane = lanes_of((count, 128)) == 0
        for v in range(NV):
            n = 0 if NS <= v < NS + 2 else 1
            main, patch = now[v, here], now[v, 0:8]
            across_patch = kept[4 + n, 0:8] * (roll(patch, -1, 1) - patch)
            seam = jnp.where(c == 1, roll(across_patch, 63, 1), across_patch)
            groups = range(low // 8 - 1, (low + count) // 8 - 1)
            closing = jnp.concatenate([roll(seam, -8 * g - 2, 1) for g in groups], axis=0)
            across = kept[4 + n, here] * (roll(main, -1, 1) - main)
            before = jnp.where(zero_lane, closing, roll(across, 1, 1))
            across = jnp.where(last_lane, closing, across)
            change = (across - before) + (
                kept[2 + n, here] * (now[v, after] - main)
                + kept[2 + n, ahead] * (now[v, ahead] - main)
            )
            if number < 2:
                down_patch = kept[2 + n, 0:8] * (patch_up(patch) - patch)
                change_patch = (across_patch - roll(across_patch, 1, 1)) + (
                    down_patch - patch_down(down_patch)
                )
                new_main = main + STEP * change
                new_patch = patch + STEP * change_patch
                if old_share:
                    new_main = old_share * first[v, here] + new_share * new_main
                    new_patch = old_share * first[v, 0:8] + new_share * new_patch
                now[v, here] = new_main
                now[v, 0:8] = new_patch
            else:
                residual[v] = change
                final[v] = old_share * first[v, here] + new_share * (main + STEP * change)

    section(0, 0.0, 1.0)
    section(1, 0.75, 0.25)
    section(2, 1.0 / 3.0, 2.0 / 3.0)


def local(species, velocity, heat, shear, thermal):
    layers = species.shape[1]
    columns = species.shape[3]
    assert (layers, columns) == (16, 128)
    rows = 2 * layers
    species = species.reshape(NS, rows, columns)
    velocity = velocity.reshape(2, rows, columns)
    heat = heat.reshape(rows, columns)
    f32 = jnp.float32
    vmem = pl.BlockSpec(memory_space=pltpu.VMEM)
    smem = pl.BlockSpec(memory_space=pltpu.SMEM)
    anywhere = pl.BlockSpec(memory_space=pl.ANY)
    tiles = NV + EDGE_TILES
    vert, side, own = pl.pallas_call(
        exchange_kernel,
        out_shape=(
            jax.ShapeDtypeStruct((2, tiles, 8, columns), f32),
            jax.ShapeDtypeStruct((6, EDGE_TILES, 8, columns), f32),
            jax.ShapeDtypeStruct((EDGE_TILES, 8, columns), f32),
        ),
        in_specs=[pl.BlockSpec(memory_space=pltpu.HBM)] * 3,
        out_specs=(anywhere,) * 3,
        scratch_shapes=[
            pltpu.VMEM((NV, rows, columns), f32),
            pltpu.VMEM((EDGE_TILES, 8, columns), f32),
            pltpu.VMEM((2, tiles, 8, columns), f32),
            pltpu.SemaphoreType.DMA((4,)),
            pltpu.SemaphoreType.DMA((2,)),
            pltpu.SemaphoreType.DMA((2,)),
            pltpu.SemaphoreType.DMA((6,)),
            pltpu.SemaphoreType.DMA((6,)),
        ],
        compiler_params=pltpu.CompilerParams(
            collective_id=0, has_side_effects=True, vmem_limit_bytes=8 * 2**20
        ),
        name="exchange",
    )(species, velocity, heat)
    shape = jax.ShapeDtypeStruct((NV, rows, columns), f32)
    final, residual = pl.pallas_call(
        sections_kernel,
        out_shape=(shape, shape),
        in_specs=[smem] * 2 + [anywhere] * 6,
        out_specs=(vmem,) * 2,
        scratch_shapes=[
            pltpu.VMEM((NV, rows + 32, columns), f32),
            pltpu.VMEM((NV, rows + 32, columns), f32),
            pltpu.VMEM((6, rows + 32, columns), f32),
            pltpu.VMEM((9, EDGE_TILES, 8, columns), f32),
            pltpu.SemaphoreType.DMA((9,)),
        ],
        compiler_params=pltpu.CompilerParams(vmem_limit_bytes=16 * 2**20),
        name="sections",
    )(shear, thermal, species, velocity, heat, vert, side, own)
    whole = (NV, layers, 2, columns)
    return final.reshape(whole), residual.reshape(whole)


def solution(mesh):
    return jax.shard_map(
        local,
        mesh=mesh,
        in_specs=(
            P(None, "wn", None, "blk"),
            P(None, "wn", None, "blk"),
            P("wn", None, "blk"),
            P(),
            P(),
        ),
        out_specs=(P(None, "wn", None, "blk"), P(None, "wn", None, "blk")),
        check_vma=False,
    )
```

time: 15.7 us -> 18.3 us (1.17)
  local copies, waits for them, and re-layouts: 0 us -> 2.4 us
    unnamed x0 -> x14, local copies, waits for them, and re-layouts: none -> 2.4 us
    pallas_call x1, Pallas kernels: 6.17 us -> 7.7 us  [local(): pl.pallas_call(sections_kernel, out_shape=(shape, shape), in_specs=[smem]...]
    pallas_call x1, Pallas kernels: 8.74 us -> 7.22 us  [local(): pl.pallas_call(exchange_kernel, out_shape=(jax.ShapeDtypeStruct((2, tiles...]
where the time goes in v3:
time: 18.3 us; the launch traced here: 18 us
  Pallas kernels  14.9 us (81%)
  local copies, waits for them, and re-layouts  2.4 us (13%)
  between operations  0.69 us (4%)
    pallas_call x1, Pallas kernels, local(): pl.pallas_call(sections_kernel, out_shape=(shape, shape), in_specs=[smem]...  7.7 us
    pallas_call x1, Pallas kernels, local(): pl.pallas_call(exchange_kernel, out_shape=(jax.ShapeDtypeStruct((2, tiles...  7.22 us
    unnamed x14, local copies, waits for them, and re-layouts  2.4 us

profile of v3, /device:TPU:0, one launch (start us, length us, event | category | flops | bytes accessed | tf_op | source)
XLA Modules:
  0.0 18.0 jit_solution(17143193065404640362)
XLA Ops:
  0.6 0.0 copy-start
  0.6 0.9 %copy-done = f32[11,16,2,128]{3,2,1,0:T(2,128)S(1)} copy-done((f32[11,16,2,128]{3,2,1,0:T(2,128)S(1)}, f32[11,16,2,128]{3,2,1,0:T(2,128)}, u32[]{:S(2)}) %copy-start) | copy-done | bytes 180248
  1.6 0.0 copy-start.2
  1.6 0.8 %copy-done.2 = f32[2,16,2,128]{3,2,1,0:T(2,128)S(1)} copy-done((f32[2,16,2,128]{3,2,1,0:T(2,128)S(1)}, f32[2,16,2,128]{3,2,1,0:T(2,128)}, u32[]{:S(2)}) %copy-start.2) | copy-done | bytes 32792
  2.3 0.0 copy-start.4
  2.3 0.7 %copy-done.4 = f32[16,2,128]{2,1,0:T(2,128)S(1)} copy-done((f32[16,2,128]{2,1,0:T(2,128)S(1)}, f32[16,2,128]{2,1,0:T(2,128)}, u32[]{:S(2)}) %copy-start.4) | copy-done | bytes 16408
  3.0 0.0 copy-start.1
  3.0 0.0 copy-start.3
  3.0 0.0 copy-start.5
  3.0 0.0 copy-start.6
  3.0 7.2 %exchange.1 = (f32[2,18,8,128]{3,2,1,0:T(8,128)S(1)}, f32[6,4,8,128]{3,2,1,0:T(8,128)S(1)}, f32[4,8,128]{2,1,0:T(8,128)S(1)}) custom-call(f32[11,32,128]{2,1,0:T(8,128)S(1)} %bitcast.5, f32[2,32,128]{2,1,0:T(8,128)S(1)} %bitcast.7, f32[32,128]{1,0:T(8,128)S(1)} %bitcast.9), custom_call_target="tpu_custom_call" | custom-call | tf_op jit(solution)/shard_map/exchange/pallas_call | solution.py:307
  10.3 0.0 copy-done.1
  10.3 0.0 copy-done.3
  10.3 0.0 copy-done.5
  10.3 0.0 copy-done.6
  10.3 7.7 %sections.1 = (f32[14,32,128]{2,1,0:T(8,128)}, f32[14,32,128]{2,1,0:T(8,128)}) custom-call(f32[11,11]{1,0:T(8,128)S(1)} %copy-done.5, f32[11,11]{1,0:T(8,128)S(1)} %copy-done.6, f32[11,32,128]{2,1,0:T(8,128)S(1)} %bitcast.6, f32[2,32,128]{2,1,0:T(8,128)S(1)} %bitcast.8, f32[32,128]{1,0:T(8,128)S(1)} %bitcast.10, ...), custom_call_target="tpu_custom_call" | custom-call | tf_op jit(solution)/shard_map/sections/pallas_call | solution.py:332
Async XLA Ops:
  0.6 0.9 %copy-start = (f32[11,16,2,128]{3,2,1,0:T(2,128)S(1)}, f32[11,16,2,128]{3,2,1,0:T(2,128)}, u32[]{:S(2)}) copy-start(f32[11,16,2,128]{3,2,1,0:T(2,128)} %param.5) | copy-start | bytes 540676
  1.6 0.8 %copy-start.2 = (f32[2,16,2,128]{3,2,1,0:T(2,128)S(1)}, f32[2,16,2,128]{3,2,1,0:T(2,128)}, u32[]{:S(2)}) copy-start(f32[2,16,2,128]{3,2,1,0:T(2,128)} %param.6) | copy-start | bytes 98308
  2.3 0.7 %copy-start.4 = (f32[16,2,128]{2,1,0:T(2,128)S(1)}, f32[16,2,128]{2,1,0:T(2,128)}, u32[]{:S(2)}) copy-start(f32[16,2,128]{2,1,0:T(2,128)} %param.7) | copy-start | bytes 49156
  3.0 7.2 %copy-start.1 = (f32[11,16,2,128]{3,2,1,0:T(2,128)S(1)}, f32[11,16,2,128]{3,2,1,0:T(2,128)}, u32[]{:S(2)}) copy-start(f32[11,16,2,128]{3,2,1,0:T(2,128)} %param.5) | copy-start | bytes 540676
  3.0 7.2 %copy-start.3 = (f32[2,16,2,128]{3,2,1,0:T(2,128)S(1)}, f32[2,16,2,128]{3,2,1,0:T(2,128)}, u32[]{:S(2)}) copy-start(f32[2,16,2,128]{3,2,1,0:T(2,128)} %param.6) | copy-start | bytes 98308
  3.0 7.3 %copy-start.5 = (f32[11,11]{1,0:T(8,128)S(1)}, f32[11,11]{1,0:T(8,128)}, u32[]{:S(2)}) copy-start(f32[11,11]{1,0:T(8,128)} %shear.1) | copy-start | bytes 1456
  3.0 7.3 %copy-start.6 = (f32[11,11]{1,0:T(8,128)S(1)}, f32[11,11]{1,0:T(8,128)}, u32[]{:S(2)}) copy-start(f32[11,11]{1,0:T(8,128)} %thermal.1) | copy-start | bytes 1456

commit v4 on v2

--- a/solution.py
+++ b/solution.py
@@ -35,7 +35,7 @@
 
 
 def exchange_kernel(
-    species, velocity, heat, vert, side, own, out_v, send_v, recv_v, send_s, recv_s
+    species, velocity, heat, vert, side, own, cells, own_v, out_v, load, send_v, recv_v, send_s, recv_s
 ):
     wn = lax.axis_index("wn")
     blk = lax.axis_index("blk")
@@ -62,13 +62,18 @@
                 barrier, inc=1, device_id=device(dw, db), device_id_type=pl.DeviceIdType.MESH
             )
 
+    loads = [
+        pltpu.make_async_copy(species, cells.at[0:NS], load.at[0]),
+        pltpu.make_async_copy(velocity, cells.at[NS:NS + 2], load.at[1]),
+        pltpu.make_async_copy(heat, cells.at[NV - 1], load.at[2]),
+    ]
+    for copy in loads:
+        copy.start()
+    for copy in loads:
+        copy.wait()
+
     def tile(v, g):
-        rows = pl.ds(8 * g, 8)
-        if v < NS:
-            return species[v, rows]
-        if v < NS + 2:
-            return velocity[v - NS, rows]
-        return heat[rows]
+        return cells[v, pl.ds(8 * g, 8)]
 
     slot = lanes_of((8, 128)) // 8
     for t in range(EDGE_TILES):
@@ -77,7 +82,7 @@
             for g in range(4):
                 at = 4 * (v % 4) + g
                 packed = jnp.where(slot == at, roll(tile(v, g), 8 * at + 3, 1), packed)
-        own[t] = packed
+        own_v[t] = packed
         out_v[0, NV + t] = packed
         out_v[1, NV + t] = packed
     for v in range(NV):
@@ -95,14 +100,17 @@
             device_id=device(dw, db), device_id_type=pl.DeviceIdType.MESH)))
     for n, (dw, db) in enumerate(SIDEWAYS):
         copies.append((dw, db, pltpu.make_async_remote_copy(
-            src_ref=own, dst_ref=side.at[n], send_sem=send_s.at[n], recv_sem=recv_s.at[n],
+            src_ref=own_v, dst_ref=side.at[n], send_sem=send_s.at[n], recv_sem=recv_s.at[n],
             device_id=device(dw, db), device_id_type=pl.DeviceIdType.MESH)))
     for dw, db, copy in copies:
         pl.when(exists(dw, db))(copy.start)
+    keep = pltpu.make_async_copy(own_v, own, load.at[3])
+    keep.start()
     for dw, db, copy in copies:
         pl.when(exists(-dw, -db))(copy.wait_recv)
     for dw, db, copy in copies:
         pl.when(exists(dw, db))(copy.wait_send)
+    keep.wait()
 
 
 def sections_kernel(
@@ -186,19 +194,12 @@
     last_lane = main_lane == 127
     zero_lane = main_lane == 0
 
-    def section(number, old_share, new_share):
+    def section(number, carry):
+        old_share = jnp.where(number == 0, 0.0, jnp.where(number == 1, 0.75, 1.0 / 3.0))
+        new_share = jnp.where(number == 0, 1.0, jnp.where(number == 1, 0.25, 2.0 / 3.0))
         for v in range(NV):
             ghost(v)
-        if number == 0:
-            cells = [now[r] for r in range(NV)]
-        else:
-            cells = [
-                jnp.concatenate(
-                    [now[r, 8:40], now[r, 48:56], jnp.where(sub >= 4, now[r, 0:8], now[r, 40:48])],
-                    axis=0,
-                )
-                for r in range(NV)
-            ]
+        cells = [now[r] for r in range(NV)]
         visc = cond = None
         for s in range(NS):
             den_visc = shear[s, 0] * cells[0]
@@ -214,13 +215,7 @@
         visc = jnp.exp(0.7 * jnp.log(temperature)) * visc
         cond = jnp.sqrt(temperature) * cond
         for n, k in enumerate((visc, cond)):
-            if number == 0:
-                kept[n] = k
-            else:
-                kept[n, 8:40] = k[0:32]
-                kept[n, 48:56] = k[32:40]
-                kept[n, 0:8] = k[40:48]
-                kept[n, 40:48] = k[40:48]
+            kept[n] = k
         for n in range(2):
             main, patch = kept[n, 0:48], kept[n, 48:56]
             kept[2 + n, 0:48] = 0.5 * (main + roll(main, -2, 0))
@@ -238,26 +233,18 @@
             across = jnp.where(last_lane, closing, across)
             down = kept[2 + n, 0:48] * (roll(main, -2, 0) - main)
             change = (across - before) + (down - roll(down, 2, 0))
-            if number < 2:
-                down_patch = kept[2 + n, 48:56] * (patch_up(patch) - patch)
-                change_patch = (across_patch - roll(across_patch, 1, 1)) + (
-                    down_patch - patch_down(down_patch)
-                )
-                new_main = main + STEP * change
-                new_patch = patch + STEP * change_patch
-                if old_share:
-                    new_main = old_share * first[v, 0:48] + new_share * new_main
-                    new_patch = old_share * first[v, 48:56] + new_share * new_patch
-                now[v, 0:48] = new_main
-                now[v, 48:56] = new_patch
-            else:
-                inner = change[8:40]
-                residual[v] = inner
-                final[v] = old_share * first[v, 8:40] + new_share * (main[8:40] + STEP * inner)
-
-    section(0, 0.0, 1.0)
-    section(1, 0.75, 0.25)
-    section(2, 1.0 / 3.0, 2.0 / 3.0)
+            down_patch = kept[2 + n, 48:56] * (patch_up(patch) - patch)
+            change_patch = (across_patch - roll(across_patch, 1, 1)) + (
+                down_patch - patch_down(down_patch)
+            )
+            new_main = old_share * first[v, 0:48] + new_share * (main + STEP * change)
+            now[v, 0:48] = new_main
+            now[v, 48:56] = old_share * first[v, 48:56] + new_share * (patch + STEP * change_patch)
+            residual[v] = change[8:40]
+            final[v] = new_main[8:40]
+        return carry
+
+    lax.fori_loop(0, 3, section, 0)
 
 
 def local(species, velocity, heat, shear, thermal):
@@ -271,6 +258,7 @@
     f32 = jnp.float32
     vmem = pl.BlockSpec(memory_space=pltpu.VMEM)
     smem = pl.BlockSpec(memory_space=pltpu.SMEM)
+    anywhere = pl.BlockSpec(memory_space=pl.ANY)
     tiles = NV + EDGE_TILES
     vert, side, own = pl.pallas_call(
         exchange_kernel,
@@ -279,10 +267,13 @@
             jax.ShapeDtypeStruct((6, EDGE_TILES, 8, columns), f32),
             jax.ShapeDtypeStruct((EDGE_TILES, 8, columns), f32),
         ),
-        in_specs=[vmem] * 3,
-        out_specs=(vmem,) * 3,
+        in_specs=[anywhere] * 3,
+        out_specs=(anywhere,) * 3,
         scratch_shapes=[
+            pltpu.VMEM((NV, rows, columns), f32),
+            pltpu.VMEM((EDGE_TILES, 8, columns), f32),
             pltpu.VMEM((2, tiles, 8, columns), f32),
+            pltpu.SemaphoreType.DMA((4,)),
             pltpu.SemaphoreType.DMA((2,)),
             pltpu.SemaphoreType.DMA((2,)),
             pltpu.SemaphoreType.DMA((6,)),

time: 15.7 us -> 14.8 us (0.943)
  Pallas kernels: 14.9 us -> 13.9 us
    pallas_call x1, Pallas kernels: 8.74 us -> 7.32 us  [local(): pl.pallas_call(exchange_kernel, out_shape=(jax.ShapeDtypeStruct((2, tiles...]
    pallas_call x1, Pallas kernels: 6.17 us -> 6.62 us  [local(): pl.pallas_call(sections_kernel, out_shape=(shape, shape), in_specs=[smem]...]
where the time goes in v4:
time: 14.8 us; the launch traced here: 14.6 us
  Pallas kernels  13.9 us (94%)
  between operations  0.64 us (4%)
    pallas_call x1, Pallas kernels, local(): pl.pallas_call(exchange_kernel, out_shape=(jax.ShapeDtypeStruct((2, tiles...  7.32 us
    pallas_call x1, Pallas kernels, local(): pl.pallas_call(sections_kernel, out_shape=(shape, shape), in_specs=[smem]...  6.62 us

profile of v4, /device:TPU:0, one launch (start us, length us, event | category | flops | bytes accessed | tf_op | source)
XLA Modules:
  0.0 14.6 jit_solution(355922608328061403)
XLA Ops:
  0.6 7.3 %exchange.1 = (f32[2,18,8,128]{3,2,1,0:T(8,128)}, f32[6,4,8,128]{3,2,1,0:T(8,128)}, f32[4,8,128]{2,1,0:T(8,128)}) custom-call(f32[11,32,128]{2,1,0:T(8,128)} %bitcast.5, f32[2,32,128]{2,1,0:T(8,128)} %bitcast.7, f32[32,128]{1,0:T(8,128)} %bitcast.9), custom_call_target="tpu_custom_call" | custom-call | tf_op jit(solution)/shard_map/exchange/pallas_call | solution.py:263
  8.0 6.6 %sections.1 = (f32[14,32,128]{2,1,0:T(8,128)}, f32[14,32,128]{2,1,0:T(8,128)}) custom-call(f32[11,11]{1,0:T(8,128)} %shear.1, f32[11,11]{1,0:T(8,128)} %thermal.1, f32[11,32,128]{2,1,0:T(8,128)} %bitcast.6, f32[2,32,128]{2,1,0:T(8,128)} %bitcast.8, f32[32,128]{1,0:T(8,128)} %bitcast.10, f32[2,18,8,128]{3,2,1,0:T(8,128)} %get-tuple-element.7.vert, ...), custom_call_target="tpu_custom_call" | custom-call | tf_op jit(solution)/shard_map/sections/pallas_call | solution.py:286

commit v5 on v2

--- a/solution.py
+++ b/solution.py
@@ -35,7 +35,7 @@
 
 
 def exchange_kernel(
-    species, velocity, heat, vert, side, own, out_v, send_v, recv_v, send_s, recv_s
+    species, velocity, heat, vert, side, own, cells, own_v, out_v, load, send_v, recv_v, send_s, recv_s
 ):
     wn = lax.axis_index("wn")
     blk = lax.axis_index("blk")
@@ -62,13 +62,18 @@
                 barrier, inc=1, device_id=device(dw, db), device_id_type=pl.DeviceIdType.MESH
             )
 
+    loads = [
+        pltpu.make_async_copy(species, cells.at[0:NS], load.at[0]),
+        pltpu.make_async_copy(velocity, cells.at[NS:NS + 2], load.at[1]),
+        pltpu.make_async_copy(heat, cells.at[NV - 1], load.at[2]),
+    ]
+    for copy in loads:
+        copy.start()
+    for copy in loads:
+        copy.wait()
+
     def tile(v, g):
-        rows = pl.ds(8 * g, 8)
-        if v < NS:
-            return species[v, rows]
-        if v < NS + 2:
-            return velocity[v - NS, rows]
-        return heat[rows]
+        return cells[v, pl.ds(8 * g, 8)]
 
     slot = lanes_of((8, 128)) // 8
     for t in range(EDGE_TILES):
@@ -77,7 +82,7 @@
             for g in range(4):
                 at = 4 * (v % 4) + g
                 packed = jnp.where(slot == at, roll(tile(v, g), 8 * at + 3, 1), packed)
-        own[t] = packed
+        own_v[t] = packed
         out_v[0, NV + t] = packed
         out_v[1, NV + t] = packed
     for v in range(NV):
@@ -95,14 +100,17 @@
             device_id=device(dw, db), device_id_type=pl.DeviceIdType.MESH)))
     for n, (dw, db) in enumerate(SIDEWAYS):
         copies.append((dw, db, pltpu.make_async_remote_copy(
-            src_ref=own, dst_ref=side.at[n], send_sem=send_s.at[n], recv_sem=recv_s.at[n],
+            src_ref=own_v, dst_ref=side.at[n], send_sem=send_s.at[n], recv_sem=recv_s.at[n],
             device_id=device(dw, db), device_id_type=pl.DeviceIdType.MESH)))
     for dw, db, copy in copies:
         pl.when(exists(dw, db))(copy.start)
+    keep = pltpu.make_async_copy(own_v, own, load.at[3])
+    keep.start()
     for dw, db, copy in copies:
         pl.when(exists(-dw, -db))(copy.wait_recv)
     for dw, db, copy in copies:
         pl.when(exists(dw, db))(copy.wait_send)
+    keep.wait()
 
 
 def sections_kernel(
@@ -271,6 +279,7 @@
     f32 = jnp.float32
     vmem = pl.BlockSpec(memory_space=pltpu.VMEM)
     smem = pl.BlockSpec(memory_space=pltpu.SMEM)
+    anywhere = pl.BlockSpec(memory_space=pl.ANY)
     tiles = NV + EDGE_TILES
     vert, side, own = pl.pallas_call(
         exchange_kernel,
@@ -279,10 +288,13 @@
             jax.ShapeDtypeStruct((6, EDGE_TILES, 8, columns), f32),
             jax.ShapeDtypeStruct((EDGE_TILES, 8, columns), f32),
         ),
-        in_specs=[vmem] * 3,
-        out_specs=(vmem,) * 3,
+        in_specs=[anywhere] * 3,
+        out_specs=(anywhere,) * 3,
         scratch_shapes=[
+            pltpu.VMEM((NV, rows, columns), f32),
+            pltpu.VMEM((EDGE_TILES, 8, columns), f32),
             pltpu.VMEM((2, tiles, 8, columns), f32),
+            pltpu.SemaphoreType.DMA((4,)),
             pltpu.SemaphoreType.DMA((2,)),
             pltpu.SemaphoreType.DMA((2,)),
             pltpu.SemaphoreType.DMA((6,)),

time: 15.7 us -> 14.3 us (0.911)
  Pallas kernels: 14.9 us -> 13.5 us
    pallas_call x1, Pallas kernels: 8.74 us -> 7.32 us  [local(): pl.pallas_call(exchange_kernel, out_shape=(jax.ShapeDtypeStruct((2, tiles...]
where the time goes in v5:
time: 14.3 us; the launch traced here: 14.1 us
  Pallas kernels  13.5 us (94%)
  between operations  0.64 us (4%)
    pallas_call x1, Pallas kernels, local(): pl.pallas_call(exchange_kernel, out_shape=(jax.ShapeDtypeStruct((2, tiles...  7.32 us
    pallas_call x1, Pallas kernels, local(): pl.pallas_call(sections_kernel, out_shape=(shape, shape), in_specs=[smem]...  6.17 us

profile of v5, /device:TPU:0, one launch (start us, length us, event | category | flops | bytes accessed | tf_op | source)
XLA Modules:
  0.0 14.1 jit_solution(593793542305730178)
XLA Ops:
  0.6 7.3 %exchange.1 = (f32[2,18,8,128]{3,2,1,0:T(8,128)}, f32[6,4,8,128]{3,2,1,0:T(8,128)}, f32[4,8,128]{2,1,0:T(8,128)}) custom-call(f32[11,32,128]{2,1,0:T(8,128)} %bitcast.5, f32[2,32,128]{2,1,0:T(8,128)} %bitcast.7, f32[32,128]{1,0:T(8,128)} %bitcast.9), custom_call_target="tpu_custom_call" | custom-call | tf_op jit(solution)/shard_map/exchange/pallas_call | solution.py:284
  8.0 6.2 %sections.1 = (f32[14,32,128]{2,1,0:T(8,128)}, f32[14,32,128]{2,1,0:T(8,128)}) custom-call(f32[11,11]{1,0:T(8,128)} %shear.1, f32[11,11]{1,0:T(8,128)} %thermal.1, f32[11,32,128]{2,1,0:T(8,128)} %bitcast.6, f32[2,32,128]{2,1,0:T(8,128)} %bitcast.8, f32[32,128]{1,0:T(8,128)} %bitcast.10, f32[2,18,8,128]{3,2,1,0:T(8,128)} %get-tuple-element.7.vert, ...), custom_call_target="tpu_custom_call" | custom-call | tf_op jit(solution)/shard_map/sections/pallas_call | solution.py:307

commit v6 on v5

--- a/solution.py
+++ b/solution.py
@@ -114,7 +114,8 @@
 
 
 def sections_kernel(
-    shear, thermal, species, velocity, heat, vert, side, own, final, residual, now, first, kept
+    shear, thermal, species, velocity, heat, vert, side, own, final, residual, now, first, kept,
+    final_v, residual_v, out
 ):
     wn = lax.axis_index("wn")
     blk = lax.axis_index("blk")
@@ -260,12 +261,22 @@
                 now[v, 48:56] = new_patch
             else:
                 inner = change[8:40]
-                residual[v] = inner
-                final[v] = old_share * first[v, 8:40] + new_share * (main[8:40] + STEP * inner)
-
+                residual_v[v] = inner
+                final_v[v] = old_share * first[v, 8:40] + new_share * (main[8:40] + STEP * inner)
+                if v in (3, 7, 10, 13):
+                    n = len(leaving)
+                    done = pl.ds((0, 4, 8, 11)[n // 2], (4, 4, 3, 3)[n // 2])
+                    for here, there in ((final_v, final), (residual_v, residual)):
+                        leaving.append(pltpu.make_async_copy(
+                            here.at[done], there.at[done], out.at[len(leaving)]))
+                        leaving[-1].start()
+
+    leaving = []
     section(0, 0.0, 1.0)
     section(1, 0.75, 0.25)
     section(2, 1.0 / 3.0, 2.0 / 3.0)
+    for copy in leaving:
+        copy.wait()
 
 
 def local(species, velocity, heat, shear, thermal):
@@ -308,11 +319,14 @@
         sections_kernel,
         out_shape=(shape, shape),
         in_specs=[smem] * 2 + [vmem] * 6,
-        out_specs=(vmem,) * 2,
+        out_specs=(anywhere,) * 2,
         scratch_shapes=[
             pltpu.VMEM((NV, rows + 24, columns), f32),
             pltpu.VMEM((NV, rows + 24, columns), f32),
             pltpu.VMEM((6, rows + 24, columns), f32),
+            pltpu.VMEM((NV, rows, columns), f32),
+            pltpu.VMEM((NV, rows, columns), f32),
+            pltpu.SemaphoreType.DMA((8,)),
         ],
         name="sections",
     )(shear, thermal, species, velocity, heat, vert, side, own)

time: 14.3 us -> 14.3 us (level)
  no operation moved by 1% of the time
where the time goes in v6:
time: 14.3 us; the launch traced here: 14.1 us
  Pallas kernels  13.5 us (94%)
  between operations  0.64 us (4%)
    pallas_call x1, Pallas kernels, local(): pl.pallas_call(exchange_kernel, out_shape=(jax.ShapeDtypeStruct((2, tiles...  7.32 us
    pallas_call x1, Pallas kernels, local(): pl.pallas_call(sections_kernel, out_shape=(shape, shape), in_specs=[smem]...  6.13 us

profile of v6, /device:TPU:0, one launch (start us, length us, event | category | flops | bytes accessed | tf_op | source)
XLA Modules:
  0.0 14.1 jit_solution(12765958294162103024)
XLA Ops:
  0.6 7.3 %exchange.1 = (f32[2,18,8,128]{3,2,1,0:T(8,128)}, f32[6,4,8,128]{3,2,1,0:T(8,128)}, f32[4,8,128]{2,1,0:T(8,128)}) custom-call(f32[11,32,128]{2,1,0:T(8,128)} %bitcast.5, f32[2,32,128]{2,1,0:T(8,128)} %bitcast.7, f32[32,128]{1,0:T(8,128)} %bitcast.9), custom_call_target="tpu_custom_call" | custom-call | tf_op jit(solution)/shard_map/exchange/pallas_call | solution.py:295
  8.0 6.1 %sections.1 = (f32[14,32,128]{2,1,0:T(8,128)}, f32[14,32,128]{2,1,0:T(8,128)}) custom-call(f32[11,11]{1,0:T(8,128)} %shear.1, f32[11,11]{1,0:T(8,128)} %thermal.1, f32[11,32,128]{2,1,0:T(8,128)} %bitcast.6, f32[2,32,128]{2,1,0:T(8,128)} %bitcast.8, f32[32,128]{1,0:T(8,128)} %bitcast.10, f32[2,18,8,128]{3,2,1,0:T(8,128)} %get-tuple-element.7.vert, ...), custom_call_target="tpu_custom_call" | custom-call | tf_op jit(solution)/shard_map/sections/pallas_call | solution.py:318
